TPU v7x, 128 devices: a whole 4x4x4 slice. The times are simulated.
128 devices in a mesh: dp: 16 (over x_lo, y, core), tensor: 8 (over z, x_hi).
Axes of the slice: x: 4 (x_hi: 2, x_lo: 2; x = x_hi * 2 + x_lo), y: 4, z: 4, core: 2. Of those that a mesh axis runs over, the one named last changes fastest.
Arguments:
- q_latent: bfloat16 [1024, 64, 576], P(('dp', 'tensor')), may hold values from -4 to 4
- kv_cache: bfloat16 [1024, 512, 576], P(('dp', 'tensor')), may hold values from -4 to 4
- new_latent: bfloat16 [1024, 576], P(('dp', 'tensor')), may hold values from -4 to 4
- cache_len: int32 [1024], P(('dp', 'tensor')), may hold values from 2 to 512, as said below
- residual: bfloat16 [1024, 4096], P('dp'), may hold values from -3 to 3
- w_uv: bfloat16 [64, 512, 128], P('tensor'), may hold values from -1 to 1
- w_out: bfloat16 [8192, 4096], P('tensor'), may hold values from -0.0625 to 0.0625
- norm_gain: float32 [4096], replicated, may hold values from 0.1 to 1.9
- routes: int32 [1024, 8], P('dp'), may hold values from 0 to 31, all different within a row; in each aligned block of 64 rows (0 to 63, 64 to 127, ...) at most 32 rows name the same one
- route_weight: float32 [1024, 8], P('dp'), may hold values from 0.05 to 0.5
- placement: int32 [32], replicated, may hold values from 0 to 47, as said below
- w_gate: bfloat16 [48, 4096, 1024], P('dp', None, 'tensor'), may hold values from -0.09375 to 0.09375
- w_up: bfloat16 [48, 4096, 1024], P('dp', None, 'tensor'), may hold values from -0.09375 to 0.09375
- w_down: bfloat16 [48, 1024, 4096], P('dp', 'tensor'), may hold values from -0.1875 to 0.1875
Outputs:
- layer_out: bfloat16 [1024, 4096], P('dp', 'tensor')
Inputs may be any that keep to these rules, and one draw needn't show every extreme that they name: `cache_len`: in every draw one row's length is exactly 512. `routes`: A row names 8 different experts; in each aligned block of 64 rows (the rows of one index of dp) no expert is named by more than 32 rows. `placement`: distinct slots; slot s belongs to index s // 3 of dp; the 3 slots of one index of dp (never the last index) serve no expert; slot 47 always serves one; some index of dp serves 3 experts.
All inputs are finite; a program needn't handle non-finite values.
Results may differ from a plain program's by a relative error of at most 0.024.
Values may be sent and summed in bfloat16 or wider, within the bound.
No kernel may reach another device: no remote copies, remote signals or barrier semaphores. Data moves between devices by JAX's collectives and lax.ppermute only.
A program may use at most 128 MiB of HBM per device.

v0:
```python
import jax
import jax.numpy as jnp
from jax import lax
from jax.sharding import PartitionSpec as P

LATENT = 512
ROPE = 64
V_HEAD = 128


NEG = -1e30


def bucket_table(route_rows, placement, capacity):
    expert_count = placement.shape[0]
    expert_ids = route_rows.reshape(-1)
    onehot = (expert_ids[:, None] == jnp.arange(expert_count, dtype=jnp.int32)[None, :]).astype(
        jnp.int32
    )
    earlier = jnp.cumsum(onehot, axis=0) - onehot
    rank_in = jnp.sum(earlier * onehot, axis=1)
    slot_ids = jnp.sum(onehot * placement[None, :], axis=1)
    return slot_ids * capacity + rank_in


def fill_buffer(row_values, bucket, bucket_count, top_count):
    wanted = jnp.arange(bucket_count, dtype=jnp.int32)
    matches = bucket[None, :] == wanted[:, None]
    row_ids = jnp.arange(bucket.shape[0], dtype=jnp.int32) // top_count
    source = jnp.sum(jnp.where(matches, row_ids[None, :], 0), axis=1)
    present = jnp.any(matches, axis=1)
    return jnp.where(present[:, None], row_values[source], jnp.zeros((), row_values.dtype))


def on_device(
    q_latent,
    kv_cache,
    new_latent,
    cache_len,
    residual,
    w_uv,
    w_out,
    norm_gain,
    routes,
    route_weight,
    placement,
    w_gate,
    w_up,
    w_down,
):
    scale_factor = (V_HEAD + ROPE) ** (-0.5)
    scores = (
        jnp.einsum("bhk,bpk->bhp", q_latent, kv_cache, preferred_element_type=jnp.float32)
        * scale_factor
    )
    own_score = (
        jnp.einsum("bhk,bk->bh", q_latent, new_latent, preferred_element_type=jnp.float32)
        * scale_factor
    )
    position = jnp.arange(kv_cache.shape[1], dtype=jnp.int32)
    in_range = position[None, None, :] < cache_len[:, None, None]
    highest = jnp.maximum(jnp.max(jnp.where(in_range, scores, NEG), axis=2), own_score)
    weights = jnp.where(in_range, jnp.exp(scores - highest[..., None]), 0.0)
    own_weight = jnp.exp(own_score - highest)
    denominator = jnp.sum(weights, axis=2) + own_weight
    summed = jnp.einsum("bhp,bpl->bhl", weights, kv_cache[:, :, :LATENT].astype(jnp.float32))
    summed = summed + own_weight[..., None] * new_latent[:, None, :LATENT].astype(jnp.float32)
    latent = (summed / denominator[..., None]).astype(jnp.bfloat16)
    head_latent = lax.all_to_all(latent, "tensor", split_axis=1, concat_axis=0, tiled=True)
    heads_out = jnp.einsum(
        "rhl,hlv->rhv", head_latent, w_uv, preferred_element_type=jnp.float32
    ).astype(jnp.bfloat16)
    projected = jnp.dot(
        heads_out.reshape(heads_out.shape[0], -1), w_out, preferred_element_type=jnp.float32
    )
    attn_out = lax.psum(projected.astype(jnp.bfloat16), "tensor")
    hidden = (
        residual.astype(jnp.float32) + lax.optimization_barrier(attn_out).astype(jnp.float32)
    ).astype(jnp.bfloat16)
    hidden_f = lax.optimization_barrier(hidden).astype(jnp.float32)
    normed = (
        hidden_f
        * lax.rsqrt(jnp.mean(hidden_f * hidden_f, axis=1, keepdims=True) + 1e-06)
        * norm_gain
    ).astype(jnp.bfloat16)
    row_count, top_count = routes.shape
    capacity = row_count // 2
    slot_dev = w_gate.shape[0]
    owners = lax.axis_size("dp")
    slot_total = owners * slot_dev
    model_width = normed.shape[1]
    columns = model_width // lax.axis_size("tensor")
    column_start = lax.axis_index("tensor") * columns
    bucket = bucket_table(routes, placement, capacity)
    outgoing = fill_buffer(normed, bucket, slot_total * capacity, top_count)
    outgoing = outgoing.reshape(owners, slot_dev, capacity, model_width)
    arrived = lax.all_to_all(outgoing, "dp", split_axis=0, concat_axis=0, tiled=True)
    gate_pre = jnp.einsum("nscd,sdf->nscf", arrived, w_gate, preferred_element_type=jnp.float32)
    up_pre = jnp.einsum("nscd,sdf->nscf", arrived, w_up, preferred_element_type=jnp.float32)
    inner_act = (jax.nn.silu(gate_pre) * up_pre).astype(jnp.bfloat16)
    partial_out = jnp.einsum(
        "nscf,sfd->nscd", inner_act, w_down, preferred_element_type=jnp.float32
    )
    expert_out = lax.psum_scatter(
        partial_out.astype(jnp.bfloat16), "tensor", scatter_dimension=3, tiled=True
    )
    returned = lax.all_to_all(expert_out, "dp", split_axis=0, concat_axis=0, tiled=True)
    flattened = returned.reshape(slot_total * capacity, columns)
    picked = flattened[bucket].reshape(row_count, top_count, columns).astype(jnp.float32)
    mixture = jnp.sum(route_weight[..., None] * picked, axis=1)
    own_hidden = lax.dynamic_slice_in_dim(hidden_f, column_start, columns, 1)
    return (own_hidden + mixture).astype(jnp.bfloat16)


def solution(mesh):
    placed = (
        P(("dp", "tensor"), None, None),
        P(("dp", "tensor"), None, None),
        P(("dp", "tensor"), None),
        P(("dp", "tensor")),
        P("dp", None),
        P("tensor", None, None),
        P("tensor", None),
        P(),
        P("dp", None),
        P("dp", None),
        P(),
        P("dp", None, "tensor"),
        P("dp", None, "tensor"),
        P("dp", "tensor", None),
    )
    return jax.shard_map(
        on_device, mesh=mesh, in_specs=placed, out_specs=P("dp", "tensor"), check_vma=False
    )
```

profile of v0, /device:TPU:1, one launch (start us, length us, event | category | flops | bytes accessed | tf_op | source)
XLA Modules:
  0.0 518.3 jit_solution(16648347573624951549)
XLA Ops:
  6.5 0.0 copy-start
  6.5 0.0 copy-start.2
  6.5 0.9 iota_compare_fusion.3
  7.4 1.0 slice_convert_fusion
  8.5 1.5 fusion.59
  10.0 3.6 select_reduce_fusion.1
  13.6 0.3 fusion.41
  14.0 0.0 copy-done.2
  14.0 0.0 copy-start.4
  14.0 0.0 copy-start.6
  14.0 1.4 divide_convert_fusion
  15.4 1.1 copy.40
  16.5 8.3 %all-to-all-start = ((bf16[8,64,512]{2,0,1:T(8,128)(2,1)}), bf16[8,64,512]{2,0,1:T(8,128)(2,1)}, u32[]{:S(2)}, u32[]{:S(2)}) async-start(bf16[8,64,512]{2,0,1:T(8,128)(2,1)} %copy.40), calls=%async_computation | async-start | bytes 1048576 | tf_op jit(solution)/shard_map/all_to_all | solution.py:69
  24.8 0.0 all-reduce.2.cloned.1.call-start
  24.9 0.0 copy-done.4
  24.9 0.1 copy.44
  25.0 0.1 eq.42
  25.1 0.1 eq.38
  25.2 1.2 reduce-window.6
  26.3 0.2 slice_reduce_fusion
  26.6 0.0 copy-done.6
  26.6 0.1 select_reduce_fusion.2
  26.7 8.9 %all-to-all-done = bf16[8,64,512]{2,0,1:T(8,128)(2,1)} async-done(((bf16[8,64,512]{2,0,1:T(8,128)(2,1)}), bf16[8,64,512]{2,0,1:T(8,128)(2,1)}, u32[]{:S(2)}, u32[]{:S(2)}) %all-to-all-start) | async-done | bytes 524320 | tf_op jit(solution)/shard_map/all_to_all | solution.py:69
  35.6 1.7 fusion.37
  37.3 0.0 copy-start.3
  37.3 5.8 %convolution_convert_fusion = bf16[64,4096]{1,0:T(8,128)(2,1)} fusion(bf16[1024,4096]{1,0:T(8,128)(2,1)} %param.20, bf16[8,8,8,128]{3,2,1,0:T(8,128)(2,1)S(1)} %fusion.37), kind=kOutput, calls=%fused_computation.8 | convolution fusion | flops 537133056 | bytes 9043968 | tf_op jit(solution)/shard_map/dot_general | solution.py:73
  43.1 0.0 all-reduce.2.cloned.1.call-update
  43.2 0.0 reduce-scatter.2.cloned.1.call-start
  43.2 0.4 fusion.9
  43.6 0.1 broadcast_in_dim.64
  43.7 0.4 select_reduce_fusion
  44.2 78.7 %all-reduce.2.cloned.1.call-done = bf16[64,4096]{1,0:T(8,128)(2,1)} async-done(((bf16[64,4096]{1,0:T(8,128)(2,1)}), bf16[64,4096]{1,0:T(8,128)(2,1)}) %all-reduce.2.cloned.1.call-update) | async-done | bytes 524304 | tf_op jit(solution)/shard_map/psum | solution.py:76
  122.9 1.3 add_convert_fusion
  124.2 0.0 copy-start.1
  124.2 0.2 multiply_reduce_fusion
  124.5 0.6 copy-done.1
  125.1 0.0 copy-done.3
  125.1 1.0 multiply_convert_fusion
  126.1 23.1 %gather_fusion = bf16[1536,4096]{1,0:T(8,128)(2,1)} fusion(bf16[64,4096]{1,0:T(8,128)(2,1)} %multiply_convert_fusion, s32[2048]{0:T(1024)S(1)} %pad_clamp_fusion), kind=kCustom, calls=%fused_computation | custom fusion | bytes 25171968 | tf_op jit(solution)/shard_map/gather | solution.py:32
  149.2 6.4 %broadcast_select_fusion = bf16[16,3,32,4096]{3,2,1,0:T(8,128)(2,1)S(1)} fusion(bf16[16,3,32,4096]{3,2,1,0:T(8,128)(2,1)} %bitcast.83, pred[16,3,32]{2,1,0:T(4,128)(4,1)S(1)} %broadcast_in_dim.64), kind=kLoop, calls=%fused_computation.3 | loop fusion | flops 6291456 | bytes 25167360 | tf_op jit(solution)/shard_map/jit(_where)/select_n | solution.py:32
  155.6 0.0 copy-start.7
  155.6 149.3 %all_to_all.28 = bf16[16,3,32,4096]{3,2,1,0:T(8,128)(2,1)} all-to-all(bf16[16,3,32,4096]{3,2,1,0:T(8,128)(2,1)S(1)} %broadcast_select_fusion), channel_id=1, replica_groups=mesh['dp'=16,'tensor'=8] {'dp'}, dimensions={0} | all-to-all | bytes 25165824 | tf_op jit(solution)/shard_map/all_to_all | solution.py:97
  304.9 0.0 copy-done.7
  304.9 7.3 %fusion.13 = f32[16,3,32,128]{3,2,0,1:T(8,128)} fusion(bf16[3,4096,128]{2,1,0:T(8,128)(2,1)S(1)} %copy-done.7, bf16[16,3,32,4096]{3,2,1,0:T(8,128)(2,1)} %all_to_all.28), kind=kOutput, calls=%fused_computation.19 | convolution fusion | flops 1610612736 | bytes 16515072 | tf_op jit(solution)/shard_map/nscd,sdf->nscf/dot_general | solution.py:98
  312.2 0.0 copy-done
  312.2 13.4 %convert_bitcast_fusion = bf16[16,3,32,4096]{3,2,0,1:T(8,128)(2,1)} fusion(bf16[3,128,4096]{2,1,0:T(8,128)(2,1)S(1)} %copy-done, bf16[3,4096,128]{2,1,0:T(8,128)(2,1)} %param.26, bf16[16,3,32,4096]{3,2,1,0:T(8,128)(2,1)} %all_to_all.28, f32[16,3,32,128]{3,2,0,1:T(8,128)} %fusion.13), kind=kOutput, calls=%fused_computation.2 | convolution fusion | flops 3228696576 | bytes 32243712 | tf_op jit(solution)/shard_map/nscf,sfd->nscd/dot_general | solution.py:101
  325.6 0.0 reduce-scatter.2.cloned.1.call-update
  325.6 0.0 copy-start.5
  325.6 148.3 %reduce-scatter.2.cloned.1.call-done = bf16[16,3,32,512]{3,2,0,1:T(8,128)(2,1)} async-done(((bf16[16,3,32,4096]{3,2,0,1:T(8,128)(2,1)}), bf16[16,3,32,512]{3,2,0,1:T(8,128)(2,1)}) %reduce-scatter.2.cloned.1.call-update) | async-done | bytes 1572880 | tf_op jit(solution)/shard_map/reduce_scatter | solution.py:104
  473.9 2.7 copy.49
  476.6 5.7 %all-to-all-start.2 = ((bf16[16,3,32,512]{3,2,1,0:T(8,128)(2,1)}), bf16[16,3,32,512]{3,2,1,0:T(8,128)(2,1)}, u32[]{:S(2)}, u32[]{:S(2)}) async-start(bf16[16,3,32,512]{3,2,1,0:T(8,128)(2,1)} %copy.49), calls=%async_computation.3 | async-start | bytes 3145728 | tf_op jit(solution)/shard_map/all_to_all | solution.py:107
  482.3 0.0 copy-done.5
  482.3 0.1 copy.43
  482.4 2.1 convert_element_type.65
  484.5 19.7 %all-to-all-done.2 = bf16[16,3,32,512]{3,2,1,0:T(8,128)(2,1)} async-done(((bf16[16,3,32,512]{3,2,1,0:T(8,128)(2,1)}), bf16[16,3,32,512]{3,2,1,0:T(8,128)(2,1)}, u32[]{:S(2)}, u32[]{:S(2)}) %all-to-all-start.2) | async-done | bytes 1572896 | tf_op jit(solution)/shard_map/all_to_all | solution.py:107
  504.2 4.3 gather_fusion.1
  508.5 1.4 fusion.38
  509.9 1.6 add_convert_fusion.1
  (11 shorter events, 0.1 us)
Async XLA Ops:
  6.5 305.7 %copy-start = (bf16[3,128,4096]{2,1,0:T(8,128)(2,1)S(1)}, bf16[3,128,4096]{2,1,0:T(8,128)(2,1)}, u32[]{:S(2)}) copy-start(bf16[3,128,4096]{2,1,0:T(8,128)(2,1)} %param.27) | copy-start | bytes 9437188
  6.5 7.4 %copy-start.2 = (bf16[8,512,576]{1,2,0:T(8,128)(2,1)S(1)}, bf16[8,512,576]{1,2,0:T(8,128)(2,1)}, u32[]{:S(2)}) copy-start(bf16[8,512,576]{1,2,0:T(8,128)(2,1)} %param.15) | copy-start | bytes 14155780
  14.0 10.9 %copy-start.4 = (s32[64,8]{0,1:T(8,128)S(1)}, s32[64,8]{0,1:T(8,128)}, u32[]{:S(2)}) copy-start(s32[64,8]{0,1:T(8,128)} %param.22) | copy-start | bytes 6148
  14.0 12.6 %copy-start.6 = (s32[32]{0:T(128)S(1)}, s32[32]{0:T(128)}, u32[]{:S(2)}) copy-start(s32[32]{0:T(128)} %param.24) | copy-start | bytes 388
  16.5 19.1 %all-to-all-start = ((bf16[8,64,512]{2,0,1:T(8,128)(2,1)}), bf16[8,64,512]{2,0,1:T(8,128)(2,1)}, u32[]{:S(2)}, u32[]{:S(2)}) async-start(bf16[8,64,512]{2,0,1:T(8,128)(2,1)} %copy.40), calls=%async_computation | async-start | bytes 1048576 | tf_op jit(solution)/shard_map/all_to_all | solution.py:69
  24.8 98.1 %all-reduce.2.cloned.1.call-start = ((), (), s32[]{:S(2)}) async-start(), calls=%async_computation.4 | async-start | bytes 1048576 | tf_op jit(solution)/shard_map/psum | solution.py:76
  37.3 87.7 %copy-start.3 = (f32[4096]{0:T(1024)S(1)}, f32[4096]{0:T(1024)}, u32[]{:S(2)}) copy-start(f32[4096]{0:T(1024)} %param.21) | copy-start | bytes 49156
  43.2 430.7 %reduce-scatter.2.cloned.1.call-start = ((), (), s32[]{:S(2)}) async-start(), calls=%async_computation.5 | async-start | bytes 14155776 | tf_op jit(solution)/shard_map/reduce_scatter | solution.py:104
  124.2 0.8 copy-start.1
  155.6 149.3 %copy-start.7 = (bf16[3,4096,128]{2,1,0:T(8,128)(2,1)S(1)}, bf16[3,4096,128]{2,1,0:T(8,128)(2,1)}, u32[]{:S(2)}) copy-start(bf16[3,4096,128]{2,1,0:T(8,128)(2,1)} %param.25) | copy-start | bytes 9437188
  325.6 156.7 %copy-start.5 = (f32[64,8]{0,1:T(8,128)S(1)}, f32[64,8]{0,1:T(8,128)}, u32[]{:S(2)}) copy-start(f32[64,8]{0,1:T(8,128)} %param.23) | copy-start | bytes 6148
  476.6 27.6 %all-to-all-start.2 = ((bf16[16,3,32,512]{3,2,1,0:T(8,128)(2,1)}), bf16[16,3,32,512]{3,2,1,0:T(8,128)(2,1)}, u32[]{:S(2)}, u32[]{:S(2)}) async-start(bf16[16,3,32,512]{3,2,1,0:T(8,128)(2,1)} %copy.49), calls=%async_computation.3 | async-start | bytes 3145728 | tf_op jit(solution)/shard_map/all_to_all | solution.py:107
Sparse Core Ops, SparseCore 0:
  43.3 79.5 all-reduce.1
  325.7 148.1 reduce-scatter.1
where the time goes:
time: 519 us; the launch traced here: 518 us
  waiting for transfers between devices  256 us (49%)
  blocking collectives  149 us (29%)
  matrix products  34.7 us (7%)
  local copies, waits for them, and re-layouts  32.5 us (6%)
  other arithmetic  18.4 us (4%)
  starting transfers between devices  14.1 us (3%)
  between operations  13.6 us (3%)
    all_to_all x1, blocking collectives, on_device(): lax.all_to_all(outgoing, 'dp', split_axis=0, concat_axis=0, tiled=True)  149 us
    reduce_scatter x1, waiting for transfers between devices, on_device(): lax.psum_scatter(partial_out.astype(jnp.bfloat16), 'tensor', scatter_dime...  148 us
    psum x1, waiting for transfers between devices, on_device(): attn_out = lax.psum(projected.astype(jnp.bfloat16), 'tensor')  78.7 us
    gather x1, local copies, waits for them, and re-layouts, fill_buffer(): row_values[source]  23.1 us
    all_to_all x1, waiting for transfers between devices, on_device(): lax.all_to_all(expert_out, 'dp', split_axis=0, concat_axis=0, tiled=True)  19.7 us
    dot_general x1, matrix products, on_device(): jnp.einsum('nscf,sfd->nscd', inner_act, w_down, preferred_element_type=jn...  13.4 us
  transfers between devices with their start and end apart: 4, of which 4 were waited for; matrix products, arithmetic and copies ran while one was open for 1% of the time, Pallas kernels for 0%

commit v1 on v0

v1 whole, which is shorter than its diff:
```python
import jax
import jax.numpy as jnp
from jax import lax
from jax.experimental import pallas as pl
from jax.experimental.pallas import tpu as pltpu
from jax.sharding import Mesh, PartitionSpec as P

LATENT = 512
ROPE = 64
V_HEAD = 128
NEG = -1e30

DP = ("xl", "y", "c")
TN = ("z", "xh")
CHIPS = ("xl", "y", "z", "xh")
SWAP = [(0, 1), (1, 0)]


def attend(q_latent, kv_cache, new_latent, cache_len):
    scale_factor = (V_HEAD + ROPE) ** (-0.5)
    scores = (
        jnp.einsum("bhk,bpk->bhp", q_latent, kv_cache, preferred_element_type=jnp.float32)
        * scale_factor
    )
    own_score = (
        jnp.einsum("bhk,bk->bh", q_latent, new_latent, preferred_element_type=jnp.float32)
        * scale_factor
    )
    position = jnp.arange(kv_cache.shape[1], dtype=jnp.int32)
    in_range = position[None, None, :] < cache_len[:, None, None]
    highest = jnp.maximum(jnp.max(jnp.where(in_range, scores, NEG), axis=2), own_score)
    weights = jnp.where(in_range, jnp.exp(scores - highest[..., None]), 0.0)
    own_weight = jnp.exp(own_score - highest)
    denominator = jnp.sum(weights, axis=2) + own_weight
    summed = jnp.einsum("bhp,bpl->bhl", weights, kv_cache[:, :, :LATENT].astype(jnp.float32))
    summed = summed + own_weight[..., None] * new_latent[:, None, :LATENT].astype(jnp.float32)
    return (summed / denominator[..., None]).astype(jnp.bfloat16)


def experts_kernel(x_ref, mix_ref, wg_ref, wu_ref, wd_ref, out_ref):
    x = x_ref[...]
    mix = mix_ref[...]
    parts = []
    for s in range(3):
        both = jnp.concatenate([wg_ref[s], wu_ref[s]], axis=1)
        pre = jnp.dot(x, both, preferred_element_type=jnp.float32)
        gate, up = pre[:, :128], pre[:, 128:]
        act = gate / (1.0 + jnp.exp(-gate)) * up * mix[:, s : s + 1]
        parts.append(act.astype(jnp.bfloat16))
    inner = jnp.concatenate(parts, axis=1)
    blocks = out_ref.shape[0]
    for t in range(8):
        w = wd_ref[:, t * 512 : (t + 1) * 512]
        piece = jnp.dot(inner, w, preferred_element_type=jnp.float32).astype(jnp.bfloat16)
        out_ref[:, t] = piece.reshape(blocks, 64, 512)


def experts(x, mix, w_gate, w_up, w_down):
    rows = x.shape[0]
    tile = 256
    return pl.pallas_call(
        experts_kernel,
        grid=(rows // tile,),
        out_shape=jax.ShapeDtypeStruct((rows // 64, 8, 64, 512), jnp.bfloat16),
        in_specs=[
            pl.BlockSpec((tile, 4096), lambda i: (i, 0)),
            pl.BlockSpec((tile, 3), lambda i: (i, 0)),
            pl.BlockSpec((3, 4096, 128), lambda i: (0, 0, 0)),
            pl.BlockSpec((3, 4096, 128), lambda i: (0, 0, 0)),
            pl.BlockSpec((384, 4096), lambda i: (0, 0)),
        ],
        out_specs=pl.BlockSpec((tile // 64, 8, 64, 512), lambda i: (i, 0, 0, 0)),
        compiler_params=pltpu.CompilerParams(vmem_limit_bytes=48 * 1024 * 1024),
        cost_estimate=pl.CostEstimate(
            flops=rows * 4096 * 384 * 6, bytes_accessed=26_000_000, transcendentals=rows * 384
        ),
    )(x, mix, w_gate, w_up, w_down.reshape(384, 4096))


def on_device(
    q_latent,
    kv_cache,
    new_latent,
    cache_len,
    residual,
    w_uv,
    w_out,
    norm_gain,
    routes,
    route_weight,
    placement,
    w_gate,
    w_up,
    w_down,
):
    core = lax.axis_index("c")
    tensor = lax.axis_index("z") * 2 + lax.axis_index("xh")
    dp = (lax.axis_index("xl") * 4 + lax.axis_index("y")) * 2 + core

    slots = jnp.sum(
        jnp.where(
            routes[:, :, None] == jnp.arange(placement.shape[0], dtype=jnp.int32),
            placement,
            0,
        ),
        axis=2,
    ).astype(jnp.float32)
    plan = lax.all_gather(jnp.concatenate([slots, route_weight], axis=1), DP, axis=0, tiled=True)
    mine = (dp * 3 + jnp.arange(3)).astype(jnp.float32)
    mix = jnp.sum(
        jnp.where(plan[:, None, :8] == mine[None, :, None], plan[:, None, 8:], 0.0), axis=2
    )
    mix = mix.reshape(8, 2, 64, 3).transpose(1, 0, 2, 3).reshape(2, 512, 3)
    mix_own = lax.dynamic_index_in_dim(mix, core, 0, keepdims=False)
    mix_other = lax.dynamic_index_in_dim(mix, 1 - core, 0, keepdims=False)

    latent = attend(q_latent, kv_cache, new_latent, cache_len)
    head_latent = lax.all_to_all(latent, TN, split_axis=1, concat_axis=0, tiled=True)
    heads_out = jnp.einsum(
        "rhl,hlv->rhv", head_latent, w_uv, preferred_element_type=jnp.float32
    ).astype(jnp.bfloat16)
    projected = jnp.dot(
        heads_out.reshape(64, -1), w_out, preferred_element_type=jnp.float32
    ).astype(jnp.bfloat16)
    terms = lax.all_to_all(projected.reshape(8, 8, 4096), TN, 0, 0, tiled=True)
    attn_out = jnp.sum(terms.astype(jnp.float32), axis=0).astype(jnp.bfloat16)
    own_rows = lax.dynamic_slice_in_dim(residual, tensor * 8, 8, 0)
    hidden = (own_rows.astype(jnp.float32) + attn_out.astype(jnp.float32)).astype(jnp.bfloat16)
    hidden_f = hidden.astype(jnp.float32)
    normed = (
        hidden_f
        * lax.rsqrt(jnp.mean(hidden_f * hidden_f, axis=1, keepdims=True) + 1e-06)
        * norm_gain
    ).astype(jnp.bfloat16)

    spread = jnp.broadcast_to(normed[None], (64, 8, 4096))
    x_own = lax.all_to_all(spread, CHIPS, 0, 0, tiled=True).reshape(512, 4096)
    x_other = lax.ppermute(x_own, "c", SWAP)
    hidden_cols = lax.all_to_all(hidden.reshape(8, 8, 512), TN, 1, 0, tiled=True).reshape(64, 512)

    p_other = experts(x_other, mix_other, w_gate, w_up, w_down)
    from_other = lax.ppermute(p_other, "c", SWAP)
    p_own = experts(x_own, mix_own, w_gate, w_up, w_down)
    both = (p_own.astype(jnp.float32) + from_other.astype(jnp.float32)).astype(jnp.bfloat16)
    back = lax.all_to_all(both.reshape(64, 64, 512), CHIPS, 0, 0, tiled=True)
    mixture = jnp.sum(back.astype(jnp.float32), axis=0)
    return (hidden_cols.astype(jnp.float32) + mixture).astype(jnp.bfloat16)


def solution(mesh):
    fine = Mesh(mesh.devices.reshape(2, 4, 2, 4, 2), ("xl", "y", "c", "z", "xh"))
    both = DP + TN
    placed = (
        P(both, None, None),
        P(both, None, None),
        P(both, None),
        P(both),
        P(DP, None),
        P(TN, None, None),
        P(TN, None),
        P(),
        P(DP, None),
        P(DP, None),
        P(),
        P(DP, None, TN),
        P(DP, None, TN),
        P(DP, TN, None),
    )
    return jax.shard_map(
        on_device, mesh=fine, in_specs=placed, out_specs=P(DP, TN), check_vma=False
    )
```

time: 519 us -> 228 us (0.44)
  waiting for transfers between devices: 256 us -> 13.4 us
  local copies, waits for them, and re-layouts: 32.5 us -> 5.24 us
  Pallas kernels: 0 us -> 25.5 us
  matrix products: 34.7 us -> 9.25 us
  between operations: 13.6 us -> 0.26 us
    reduce_scatter x1 -> x0, waiting for transfers between devices: 148 us -> none  [on_device(): lax.psum_scatter(partial_out.astype(jnp.bfloat16), 'tensor', scatter_dime...]
    psum x1 -> x0, waiting for transfers between devices: 78.7 us -> none  [on_device(): attn_out = lax.psum(projected.astype(jnp.bfloat16), 'tensor')]
    gather x2 -> x0, local copies, waits for them, and re-layouts: 27.4 us -> none  [the longest x1 23.1 us: fill_buffer(): row_values[source]]
    pallas_call x0 -> x2, Pallas kernels: none -> 25.5 us  [experts(): pl.pallas_call(experts_kernel, grid=(rows // tile,), out_shape=jax.ShapeD...]
    dot_general x6 -> x4, matrix products: 33 us -> 8.94 us  [the longest x1 3.73 us: attend(): jnp.einsum('bhk,bpk->bhp', q_latent, kv_cache, preferred_element_type=jnp...]
    all_to_all x1 -> x3, blocking collectives: 149 us -> 130 us  [the longest x1 55.5 us: on_device(): back = lax.all_to_all(both.reshape(64, 64, 512), CHIPS, 0, 0, tiled=True)]
    all_gather x0 -> x1, blocking collectives: none -> 17.6 us  [on_device(): lax.all_gather(jnp.concatenate([slots, route_weight], axis=1), DP, axis=0...]
    all_to_all x2, waiting for transfers between devices: 28.6 us -> 13.4 us  [the longest x1 9.39 us: on_device(): terms = lax.all_to_all(projected.reshape(8, 8, 4096), TN, 0, 0, tiled=True)]
  transfers between devices with their start and end apart: 4 -> 4, of which waited for: 4 -> 2; matrix products, arithmetic and copies ran while one was open for 1% -> 2% of each run, Pallas kernels for 0% -> 6%
where the time goes in v1:
time: 228 us; the launch traced here: 226 us
  blocking collectives  147 us (64%)
  Pallas kernels  25.5 us (11%)
  other arithmetic  13.6 us (6%)
  waiting for transfers between devices  13.4 us (6%)
  starting transfers between devices  11.6 us (5%)
  matrix products  9.25 us (4%)
  local copies, waits for them, and re-layouts  5.24 us (2%)
    all_to_all x1, blocking collectives, on_device(): back = lax.all_to_all(both.reshape(64, 64, 512), CHIPS, 0, 0, tiled=True)  55.5 us
    all_to_all x1, blocking collectives, on_device(): x_own = lax.all_to_all(spread, CHIPS, 0, 0, tiled=True).reshape(512, 4096)  55.5 us
    pallas_call x2, Pallas kernels, experts(): pl.pallas_call(experts_kernel, grid=(rows // tile,), out_shape=jax.ShapeD...  25.5 us
    all_to_all x1, blocking collectives, on_device(): lax.all_to_all(latent, TN, split_axis=1, concat_axis=0, tiled=True)  18.8 us
    all_gather x1, blocking collectives, on_device(): lax.all_gather(jnp.concatenate([slots, route_weight], axis=1), DP, axis=0...  17.6 us
    all_to_all x1, waiting for transfers between devices, on_device(): terms = lax.all_to_all(projected.reshape(8, 8, 4096), TN, 0, 0, tiled=True)  9.39 us
    convert_element_type x1, other arithmetic, on_device(): (p_own.astype(jnp.float32) + from_other.astype(jnp.float32)).astype(jnp.b...  5.09 us
  transfers between devices with their start and end apart: 4, of which 2 were waited for; matrix products, arithmetic and copies ran while one was open for 2% of the time, Pallas kernels for 6%

profile of v1, /device:TPU:1, one launch (start us, length us, event | category | flops | bytes accessed | tf_op | source)
XLA Modules:
  0.0 226.2 jit_solution(7419876894389202265)
XLA Ops:
  0.0 0.0 copy-start
  0.0 0.0 copy-start.3
  0.0 0.9 iota_compare_fusion.1
  0.9 1.0 slice_convert_fusion
  1.9 1.4 fusion.21
  3.3 0.0 slice-start
  3.3 3.7 %select_reduce_fusion = (f32[8,64]{1,0:T(8,128)S(1)}, f32[8,64,512]{2,1,0:T(8,128)S(1)}) fusion(pred[8,512]{1,0:T(8,128)(4,1)S(1)} %iota_compare_fusion.1, bf16[8,64,576]{2,1,0:T(8,128)(2,1)} %param.14, bf16[8,512,576]{1,2,0:T(8,128)(2,1)} %param.15), kind=kOutput, calls=%fused_computation.12 | convolution fusion | flops 302775808 | bytes 6363136 | tf_op jit(solution)/shard_map/bhk,bpk->bhp/dot_general | solution.py:22
  7.0 0.3 fusion.9
  7.4 0.0 copy-done.3
  7.4 0.0 slice-start.1
  7.4 1.4 divide_convert_fusion
  8.8 0.3 copy.47
  9.1 18.8 %all_to_all.42 = bf16[8,64,512]{2,0,1:T(8,128)(2,1)S(1)} all-to-all(bf16[8,64,512]{2,0,1:T(8,128)(2,1)S(1)} %copy.47), channel_id=1, replica_groups=mesh['xl'=2,'y'=4,'c'=2,'z'=4,'xh'=2] {'z','xh'}, dimensions={1} | all-to-all | bytes 1048576 | tf_op jit(solution)/shard_map/all_to_all | solution.py:118
  27.9 0.0 copy-done
  27.9 0.3 fusion.6
  28.2 0.0 slice-done
  28.2 0.0 slice-done.1
  28.3 0.0 copy-start.4
  28.3 2.4 %fusion = bf16[8,8,4096]{2,1,0:T(8,128)(2,1)} fusion(bf16[1024,4096]{1,0:T(8,128)(2,1)S(1)} %bitcast.51, bf16[8,8,8,128]{3,2,1,0:T(8,128)(2,1)S(1)} %fusion.6), kind=kOutput, calls=%fused_computation.3 | convolution fusion | flops 537133056 | bytes 9043968 | tf_op jit(solution)/shard_map/dot_general | solution.py:122
  30.7 3.5 %all-to-all-start.1 = ((bf16[8,8,4096]{2,1,0:T(8,128)(2,1)}), bf16[8,8,4096]{2,1,0:T(8,128)(2,1)S(1)}, u32[]{:S(2)}, u32[]{:S(2)}) async-start(bf16[8,8,4096]{2,1,0:T(8,128)(2,1)} %fusion), calls=%async_computation.1 | async-start | bytes 1048576 | tf_op jit(solution)/shard_map/all_to_all | solution.py:125
  34.2 9.4 %all-to-all-done.1 = bf16[8,8,4096]{2,1,0:T(8,128)(2,1)S(1)} async-done(((bf16[8,8,4096]{2,1,0:T(8,128)(2,1)}), bf16[8,8,4096]{2,1,0:T(8,128)(2,1)S(1)}, u32[]{:S(2)}, u32[]{:S(2)}) %all-to-all-start.1) | async-done | bytes 524320 | tf_op jit(solution)/shard_map/all_to_all | solution.py:125
  43.6 0.1 reduce_sum.58
  43.7 1.6 fusion.15
  45.3 0.0 copy-done.4
  45.3 0.9 fusion.17
  46.2 0.5 broadcast_in_dim.60
  46.7 0.0 copy-start.5
  46.7 0.0 copy-start.7
  46.7 0.0 copy-start.6
  46.8 55.5 %all_to_all.43 = bf16[64,8,4096]{2,1,0:T(8,128)(2,1)} all-to-all(bf16[64,8,4096]{2,1,0:T(8,128)(2,1)S(1)} %broadcast_in_dim.60), channel_id=1, replica_groups=mesh['xl'=2,'y'=4,'c'=2,'z'=4,'xh'=2] {'xl','y','z','xh'}, dimensions={0} | all-to-all | bytes 8388608 | tf_op jit(solution)/shard_map/all_to_all | solution.py:137
  102.2 4.5 %collective-permute-start = (bf16[512,4096]{1,0:T(8,128)(2,1)}, bf16[512,4096]{1,0:T(8,128)(2,1)}, u32[]{:S(2)}, u32[]{:S(2)}) collective-permute-start(bf16[512,4096]{1,0:T(8,128)(2,1)} %bitcast.12.x_ref), channel_id=1, source_target_pairs={{0,8},{8,0},{1,9},{9,1},{2,10},{10,2},{3,11},{11,3},{4,12},{12,4},... | collective-permute-start | bytes 12582920 | tf_op jit(solution)/shard_map/ppermute | solution.py:138
  106.7 0.0 copy-done.5
  106.7 0.0 copy-done.7
  106.7 0.1 select_reduce_fusion.1
  106.8 0.0 copy-done.6
  106.8 17.6 %all-gather = f32[16,64,16]{1,2,0:T(8,128)S(1)} all-gather(f32[1,64,16]{1,2,0:T(8,128)S(1)} %maximum_bitcast_fusion), channel_id=1, replica_groups=mesh['xl'=2,'y'=4,'c'=2,'z'=4,'xh'=2] {'xl','y','c'}, dimensions={0}, use_global_device_ids=true | all-gather | bytes 69632 | tf_op jit(solution)/shard_map/all_gather | solution.py:108
  124.5 0.1 reshape.86
  124.6 0.1 select_reduce_fusion.2
  124.7 0.1 reshape.79
  124.9 0.1 reshape.80
  125.0 0.1 copy.53
  125.1 0.0 collective-permute-done.x_ref
  125.1 0.0 copy-start.1
  125.1 1.9 copy-done.1
  127.0 12.8 %shard_map.137 = bf16[8,8,64,512]{3,2,1,0:T(8,128)(2,1)} custom-call(bf16[512,4096]{1,0:T(8,128)(2,1)} %collective-permute-done.x_ref, f32[512,3]{1,0:T(8,128)S(1)} %bitcast.48, bf16[3,4096,128]{2,1,0:T(8,128)(2,1)S(1)} %copy-done.1, bf16[3,4096,128]{2,1,0:T(8,128)(2,1)} %wu_ref.3, bf16[384,4096]{1,0:T(8,128)(2,1)} %bitcast.53), custom_call_target="tpu_custom_call" | custom-call | flops 4831838208 | bytes 26000000 | tf_op jit(solution)/shard_map/pallas_call | solution.py:61
  139.8 0.2 collective-permute-start.1
  140.0 0.1 copy.52
  140.1 0.0 copy-start.2
  140.1 1.9 copy-done.2
  142.0 12.8 %shard_map.136 = bf16[8,8,64,512]{3,2,1,0:T(8,128)(2,1)} custom-call(bf16[512,4096]{1,0:T(8,128)(2,1)} %bitcast.12.x_ref, f32[512,3]{1,0:T(8,128)S(1)} %bitcast.49, bf16[3,4096,128]{2,1,0:T(8,128)(2,1)S(1)} %copy-done.2, bf16[3,4096,128]{2,1,0:T(8,128)(2,1)} %wu_ref.3, bf16[384,4096]{1,0:T(8,128)(2,1)} %bitcast.54), custom_call_target="tpu_custom_call" | custom-call | flops 4831838208 | bytes 26000000 | tf_op jit(solution)/shard_map/pallas_call | solution.py:61
  154.8 0.0 collective-permute-done.1
  154.8 5.1 %add_convert_fusion = bf16[8,8,64,512]{3,2,1,0:T(8,128)(2,1)S(1)} fusion(bf16[8,8,64,512]{3,2,1,0:T(8,128)(2,1)} %collective-permute-done.1, bf16[8,8,64,512]{3,2,1,0:T(8,128)(2,1)} %shard_map.136), kind=kLoop, calls=%fused_computation.1 | loop fusion | flops 8388608 | bytes 12582912 | tf_op jit(solution)/shard_map/convert_element_type | solution.py:144
  159.9 55.5 %all_to_all.44 = bf16[64,64,512]{2,1,0:T(8,128)(2,1)} all-to-all(bf16[64,64,512]{2,1,0:T(8,128)(2,1)S(1)} %bitcast.52), channel_id=1, replica_groups=mesh['xl'=2,'y'=4,'c'=2,'z'=4,'xh'=2] {'xl','y','z','xh'}, dimensions={0} | all-to-all | bytes 8388608 | tf_op jit(solution)/shard_map/all_to_all | solution.py:145
  215.3 3.5 %all-to-all-start.2 = ((bf16[8,8,512]{2,0,1:T(8,128)(2,1)}), bf16[8,8,512]{2,0,1:T(8,128)(2,1)S(1)}, u32[]{:S(2)}, u32[]{:S(2)}) async-start(bf16[8,8,512]{2,0,1:T(8,128)(2,1)} %bitcast.8), calls=%async_computation.2 | async-start | bytes 131072 | tf_op jit(solution)/shard_map/all_to_all | solution.py:139
  218.8 2.8 %convert_reduce_fusion = f32[64,512]{1,0:T(8,128)S(1)} fusion(bf16[64,64,512]{2,1,0:T(8,128)(2,1)} %all_to_all.44), kind=kLoop, calls=%fused_computation | loop fusion | flops 4161536 | bytes 4325376 | tf_op jit(solution)/shard_map/reduce_sum | solution.py:146
  221.6 4.0 %all-to-all-done.2 = bf16[8,8,512]{2,0,1:T(8,128)(2,1)S(1)} async-done(((bf16[8,8,512]{2,0,1:T(8,128)(2,1)}), bf16[8,8,512]{2,0,1:T(8,128)(2,1)S(1)}, u32[]{:S(2)}, u32[]{:S(2)}) %all-to-all-start.2) | async-done | bytes 65568 | tf_op jit(solution)/shard_map/all_to_all | solution.py:139
  225.6 0.6 fusion.20
  (11 shorter events, 0.1 us)
Async XLA Ops:
  0.0 27.9 %copy-start = (bf16[8,512,128]{2,1,0:T(8,128)(2,1)S(1)}, bf16[8,512,128]{2,1,0:T(8,128)(2,1)}, u32[]{:S(2)}) copy-start(bf16[8,512,128]{2,1,0:T(8,128)(2,1)} %param.19) | copy-start | bytes 3145732
  0.0 7.4 %copy-start.3 = (bf16[8,512,576]{1,2,0:T(8,128)(2,1)S(1)}, bf16[8,512,576]{1,2,0:T(8,128)(2,1)}, u32[]{:S(2)}) copy-start(bf16[8,512,576]{1,2,0:T(8,128)(2,1)} %param.15) | copy-start | bytes 14155780
  3.3 25.0 %slice-start = ((s8[8388608]{0:T(1024)(128)(4,1)}), s8[4194304]{0:T(1024)(128)(4,1)S(1)}, s32[]{:S(2)}) async-start(s8[8388608]{0:T(1024)(128)(4,1)} %bitcast.50), calls=%async_computation.5 | async-start | bytes 8388608
  7.4 20.9 %slice-start.1 = ((s8[8388608]{0:T(1024)(128)(4,1)}), s8[4194304]{0:T(1024)(128)(4,1)S(1)}, s32[]{:S(2)}) async-start(s8[8388608]{0:T(1024)(128)(4,1)} %bitcast.50), calls=%async_computation.6 | async-start | bytes 8388608
  28.3 17.0 %copy-start.4 = (f32[4096]{0:T(1024)S(1)}, f32[4096]{0:T(1024)}, u32[]{:S(2)}) copy-start(f32[4096]{0:T(1024)} %param.21) | copy-start | bytes 49156
  30.7 12.9 %all-to-all-start.1 = ((bf16[8,8,4096]{2,1,0:T(8,128)(2,1)}), bf16[8,8,4096]{2,1,0:T(8,128)(2,1)S(1)}, u32[]{:S(2)}, u32[]{:S(2)}) async-start(bf16[8,8,4096]{2,1,0:T(8,128)(2,1)} %fusion), calls=%async_computation.1 | async-start | bytes 1048576 | tf_op jit(solution)/shard_map/all_to_all | solution.py:125
  46.7 60.0 %copy-start.5 = (s32[64,8]{0,1:T(8,128)S(1)}, s32[64,8]{0,1:T(8,128)}, u32[]{:S(2)}) copy-start(s32[64,8]{0,1:T(8,128)} %param.22) | copy-start | bytes 6148
  46.7 60.0 %copy-start.7 = (s32[32]{0:T(128)S(1)}, s32[32]{0:T(128)}, u32[]{:S(2)}) copy-start(s32[32]{0:T(128)} %param.24) | copy-start | bytes 388
  46.7 60.1 %copy-start.6 = (f32[64,8]{0,1:T(8,128)S(1)}, f32[64,8]{0,1:T(8,128)}, u32[]{:S(2)}) copy-start(f32[64,8]{0,1:T(8,128)} %param.23) | copy-start | bytes 6148
  102.2 22.9 %collective-permute-start = (bf16[512,4096]{1,0:T(8,128)(2,1)}, bf16[512,4096]{1,0:T(8,128)(2,1)}, u32[]{:S(2)}, u32[]{:S(2)}) collective-permute-start(bf16[512,4096]{1,0:T(8,128)(2,1)} %bitcast.12.x_ref), channel_id=1, source_target_pairs={{0,8},{8,0},{1,9},{9,1},{2,10},{10,2},{3,11},{11,3},{4,12},{12,4},... | collective-permute-start | bytes 12582920 | tf_op jit(solution)/shard_map/ppermute | solution.py:138
  125.1 1.9 copy-start.1
  139.8 15.0 %collective-permute-start.1 = (bf16[8,8,64,512]{3,2,1,0:T(8,128)(2,1)}, bf16[8,8,64,512]{3,2,1,0:T(8,128)(2,1)}, u32[]{:S(2)}, u32[]{:S(2)}) collective-permute-start(bf16[8,8,64,512]{3,2,1,0:T(8,128)(2,1)} %shard_map.137), channel_id=1, source_target_pairs={{0,8},{8,0},{1,9},{9,1},{2,10},{10,2},{3,11},{11,3},{4,12},{12,4},... | collective-permute-start | bytes 12582920 | tf_op jit(solution)/shard_map/ppermute | solution.py:142
  140.1 1.9 copy-start.2
  215.3 10.3 %all-to-all-start.2 = ((bf16[8,8,512]{2,0,1:T(8,128)(2,1)}), bf16[8,8,512]{2,0,1:T(8,128)(2,1)S(1)}, u32[]{:S(2)}, u32[]{:S(2)}) async-start(bf16[8,8,512]{2,0,1:T(8,128)(2,1)} %bitcast.8), calls=%async_computation.2 | async-start | bytes 131072 | tf_op jit(solution)/shard_map/all_to_all | solution.py:139
